TPU v7x, 32 devices: a whole 2x2x4 slice. The times are simulated.
32 devices in a mesh: row: 8 (over y, x, core), col: 4 (over z).
Axes of the slice: x: 2, y: 2, z: 4, core: 2. Of those that a mesh axis runs over, the one named last changes fastest.
Arguments:
- features: bfloat16 [16384, 1024], P(('row', 'col')), may hold values from 0 to 4, as said below
- coords: float32 [64, 16384], P(None, ('row', 'col')), may hold values from -1 to 1
Outputs:
- placed: float32 [64, 16384], P(None, ('row', 'col'))
- row_stress: float32 [16384], P(('row', 'col'))
- stress_norm: float32 [], replicated
Inputs may be any that keep to these rules, and one draw needn't show every extreme that they name: `features`: every molecule has at least one nonzero feature.
All inputs are finite; a program needn't handle non-finite values.
Results may differ from a plain program's by a relative error of at most 0.0003.
Values may be sent and summed in bfloat16 or wider, within the bound.
A program may use at most 192 MiB of HBM per device.

v0:
```python
import jax
import jax.numpy as jnp
from jax import lax
from jax.sharding import PartitionSpec as P

ITERS = 2
FLOOR = 0.25
EXACT = lax.Precision.HIGHEST


def from_root(block, axis, owner):
    block = jnp.where(lax.axis_index(axis) == owner, block, jnp.zeros_like(block))
    return lax.psum(block, axis)


def squares_of(values):
    return jnp.einsum("rf,rf->r", values, values, preferred_element_type=jnp.float32)


def tanimoto(left_rows, left_sq, right_rows):
    right_sq = squares_of(right_rows)
    common = lax.dot_general(
        left_rows, right_rows, (((1,), (1,)), ((), ())), preferred_element_type=jnp.float32
    )
    return 1.0 - common / (left_sq[:, None] + right_sq[None, :] - common)


def guttman_terms(dissim, x_rows, x_cols):
    coord_dim, row_len = x_rows.shape
    block_len = min(512, row_len)
    block_count = row_len // block_len
    col_norms = jnp.sum(x_cols * x_cols, axis=0)
    dis_blocks = dissim.reshape(block_count, block_len, dissim.shape[1])
    x_blocks = jnp.moveaxis(x_rows.reshape(coord_dim, block_count, block_len), 1, 0)

    def one_block(inputs):
        dis_blk, x_blk = inputs
        blk_norms = jnp.sum(x_blk * x_blk, axis=0)
        inner = lax.dot_general(
            x_blk,
            x_cols,
            (((0,), (0,)), ((), ())),
            precision=EXACT,
            preferred_element_type=jnp.float32,
        )
        distance = jnp.sqrt(
            jnp.maximum(blk_norms[:, None] + col_norms[None, :] - 2.0 * inner, FLOOR * FLOOR)
        )
        ratios = dis_blk / distance
        pulled = lax.dot_general(
            x_cols,
            ratios,
            (((1,), (1,)), ((), ())),
            precision=EXACT,
            preferred_element_type=jnp.float32,
        )
        pull_terms = x_blk * jnp.sum(ratios, axis=1)[None, :] - pulled
        stress = jnp.sum(jnp.square(dis_blk - distance), axis=1)
        return (pull_terms, stress)

    pull_terms, stress = lax.map(one_block, (dis_blocks, x_blocks))
    return (jnp.moveaxis(pull_terms, 0, 1).reshape(coord_dim, row_len), stress.reshape(row_len))


def on_device(features, coords):
    rows_n = lax.axis_size("row")
    cols_n = lax.axis_size("col")
    row_at = lax.axis_index("row")
    col_at = lax.axis_index("col")
    ratio_k = rows_n // cols_n
    share_len = coords.shape[1]
    row_len = share_len * cols_n
    molecules = row_len * rows_n
    feature_rows = lax.all_gather(features, "col", axis=0, tiled=True)
    rows_sq = squares_of(feature_rows)
    pieces = []
    for offset in range(ratio_k):
        feature_cols = from_root(feature_rows, "row", col_at * ratio_k + offset)
        pieces.append(tanimoto(feature_rows, rows_sq, feature_cols))
    dissim = jnp.concatenate(pieces, axis=1)
    dissim_sq = jnp.sum(dissim * dissim)
    current = coords
    row_stress = jnp.zeros((share_len,), jnp.float32)
    for sweep in range(ITERS):
        everything = lax.all_gather(current, ("row", "col"), axis=1, tiled=True)
        x_rows = lax.dynamic_slice_in_dim(everything, row_at * row_len, row_len, 1)
        x_cols = lax.dynamic_slice_in_dim(
            everything, col_at * row_len * ratio_k, row_len * ratio_k, 1
        )
        pull_terms, stress = guttman_terms(dissim, x_rows, x_cols)
        new_share, stress_share = (
            lax.psum_scatter(pull_terms, "col", scatter_dimension=1, tiled=True),
            lax.psum_scatter(stress, "col", scatter_dimension=0, tiled=True),
        )
        current = new_share / molecules
        row_stress = stress_share / molecules
    local_stress = jnp.sum(row_stress)
    stress_total, dissim_total = lax.psum((local_stress, dissim_sq), ("row", "col"))
    stress_norm = molecules * stress_total / dissim_total
    return (current, row_stress, stress_norm)


def solution(mesh):
    return jax.shard_map(
        on_device,
        mesh=mesh,
        in_specs=(P(("row", "col"), None), P(None, ("row", "col"))),
        out_specs=(P(None, ("row", "col")), P(("row", "col")), P()),
        check_vma=False,
    )
```

profile of v0, /device:TPU:0, one launch (start us, length us, event | category | flops | bytes accessed | tf_op | source)
XLA Modules:
  0.0 698.3 jit_solution(13126097829784607838)
XLA Ops:
  7.2 0.7 all-gather.6.cloned.1.call-update
  7.9 0.7 all-gather.4.cloned.1.call-update
  8.7 84.4 %all-gather.6.cloned.1.call-done = bf16[2048,1024]{1,0:T(8,128)(2,1)} async-done(((bf16[512,1024]{1,0:T(8,128)(2,1)}), bf16[2048,1024]{1,0:T(8,128)(2,1)}) %all-gather.6.cloned.1.call-update) | async-done | bytes 4194320 | tf_op jit(solution)/shard_map/all_gather | solution.py:74
  93.1 6.0 broadcast_select_fusion.1
  99.1 3.1 fusion.13
  102.2 54.3 %all-gather.4.cloned.1.call-done = f32[64,16384]{1,0:T(8,128)} async-done(((f32[64,512]{1,0:T(8,128)}), f32[64,16384]{1,0:T(8,128)}) %all-gather.4.cloned.1.call-update) | async-done | bytes 4194320 | tf_op jit(solution)/shard_map/all_gather | solution.py:85
  156.5 1.1 constant_dynamic-slice_fusion.5
  157.5 0.4 reshape.34
  157.9 1.4 multiply_reduce_fusion.4
  159.3 126.3 %all-reduce.5.cloned.1.call-done = (bf16[2048,1024]{1,0:T(8,128)(2,1)}, bf16[2048,1024]{1,0:T(8,128)(2,1)}) async-done(((bf16[2048,1024]{1,0:T(8,128)(2,1)}, bf16[2048,1024]{1,0:T(8,128)(2,1)}), (bf16[2048,1024]{1,0:T(8,128)(2,1)}, bf16[2048,1024]{1,0:T(8,128)(2,1)})) %all-reduce.5.cloned.1.call-update) | async-done | bytes 8388624 | tf_op jit(solution)/shard_map/psum | solution.py:13
  285.5 5.3 fusion.11
  290.9 11.4 %fusion.9 = f32[2048,2048]{0,1:T(8,128)S(1)} fusion(bf16[2048,1024]{1,0:T(8,128)(2,1)} %get-tuple-element.146, bf16[2048,1024]{1,0:T(8,128)(2,1)S(1)} %copy-done, f32[2048]{0:T(1024)S(1)} %get-tuple-element.161, f32[2048]{0:T(1024)S(1)} %fusion.13), kind=kOutput, calls=%fused_computation.25 | convolution fusion | flops 8606711808 | bytes 25182208 | tf_op jit(solution)/shard_map/dot_general | solution.py:22
  302.3 14.4 %fusion.10 = f32[2048,2048]{0,1:T(8,128)} fusion(bf16[2048,1024]{1,0:T(8,128)(2,1)} %get-tuple-element.145, bf16[2048,1024]{1,0:T(8,128)(2,1)S(1)} %copy-done, f32[2048]{0:T(1024)S(1)} %get-tuple-element.160, f32[2048]{0:T(1024)S(1)} %fusion.13), kind=kOutput, calls=%fused_computation.26 | convolution fusion | flops 8606711808 | bytes 25182208 | tf_op jit(solution)/shard_map/dot_general | solution.py:22
  316.7 20.2 %multiply_reduce_fusion.2 = (f32[]{:T(128)}, f32[2048,4096]{0,1:T(8,128)}) fusion(f32[2048,2048]{0,1:T(8,128)} %fusion.10, f32[2048,2048]{0,1:T(8,128)S(1)} %fusion.9), kind=kLoop, calls=%fused_computation.22 | loop fusion | flops 25165824 | bytes 67108864 | tf_op jit(solution)/shard_map/reduce_sum | solution.py:81
  336.9 31.1 %copy.33 = f32[2048,4096]{1,0:T(8,128)} copy(f32[2048,4096]{0,1:T(8,128)} %get-tuple-element.157) | data formatting | bytes 67108864 | tf_op jit(solution)/shard_map/while | solution.py:61
  368.0 78.5 %while.22 = (s32[]{:T(128)}, f32[4,64,512]{2,1,0:T(8,128)S(1)}, f32[4,64,512]{2,0,1:T(4,128)S(1)}, f32[4,512,4096]{2,1,0:T(8,128)}, f32[4096]{0:T(1024)S(1)}, /*index=5*/f32[64,4096]{1,0:T(8,128)S(1)}, s32[]{:T(128)}) while((s32[]{:T(128)}, f32[4,64,512]{2,1,0:T(8,128)S(1)}, f32[4,64,512]{2,0,1:T(4,128)S(1)}, f32[4,512,4096]{2,1,0:T(8,128)}, ...), condition=%wide.region_6.7_spmd, body=%wide.region_3.6_spmd.sunk | while | flops 3233938432 | bytes 28074072 | solution.py:61
  368.4 11.1 %fusion.37 = (f32[512]{0:T(512)S(1)}, f32[512,4096]{1,0:T(8,128)S(1)}) fusion(f32[64,4096]{1,0:T(8,128)S(1)} %get-tuple-element.271, f32[1,64,512]{2,0,1:T(1,128)S(1)} %constant_dynamic-slice_fusion.10, f32[4096]{0:T(1024)S(1)} %get-tuple-element.270, f32[512]{0:T(512)S(1)} %multiply_reduce_fusion.7, f32[4,512,4096]{2,1,0:T(8,128)} %get-tuple-element.269, ...), kind=kOutput, calls=%fused_computation.45.clone.1 | convolution fusion | flops 1623195136 | bytes 17977348 | tf_op jit(solution)/shard_map/while/body/eval_jaxpr/dot_general | solution.py:39
  379.6 8.2 %fusion.38 = f32[4,64,512]{2,1,0:T(8,128)S(1)} fusion(f32[4,64,512]{2,1,0:T(8,128)S(1)} %get-tuple-element.260, s32[]{:T(128)} %get-tuple-element.259, f32[512,4096]{1,0:T(8,128)S(1)} %get-tuple-element.240, f32[64,4096]{1,0:T(8,128)S(1)} %get-tuple-element.271, f32[1,64,512]{2,0,1:T(1,128)S(1)} %constant_dynamic-slice_fusion.10, ...), kind=kOutput, calls=%fused_computation.4.clone.1 | convolution fusion | flops 1610678272 | bytes 9701380 | tf_op jit(solution)/shard_map/while/body/eval_jaxpr/dot_general | solution.py:50
  387.8 0.1 constant_dynamic-slice_fusion.10
  388.0 11.1 %fusion.37 = (f32[512]{0:T(512)S(1)}, f32[512,4096]{1,0:T(8,128)S(1)}) fusion(f32[64,4096]{1,0:T(8,128)S(1)} %get-tuple-element.271, f32[1,64,512]{2,0,1:T(1,128)S(1)} %constant_dynamic-slice_fusion.10, f32[4096]{0:T(1024)S(1)} %get-tuple-element.270, f32[512]{0:T(512)S(1)} %multiply_reduce_fusion.7, f32[4,512,4096]{2,1,0:T(8,128)} %get-tuple-element.269, ...), kind=kOutput, calls=%fused_computation.45.clone.1 | convolution fusion | flops 1623195136 | bytes 17977348 | tf_op jit(solution)/shard_map/while/body/eval_jaxpr/dot_general | solution.py:39
  399.1 8.2 %fusion.38 = f32[4,64,512]{2,1,0:T(8,128)S(1)} fusion(f32[4,64,512]{2,1,0:T(8,128)S(1)} %get-tuple-element.260, s32[]{:T(128)} %get-tuple-element.259, f32[512,4096]{1,0:T(8,128)S(1)} %get-tuple-element.240, f32[64,4096]{1,0:T(8,128)S(1)} %get-tuple-element.271, f32[1,64,512]{2,0,1:T(1,128)S(1)} %constant_dynamic-slice_fusion.10, ...), kind=kOutput, calls=%fused_computation.4.clone.1 | convolution fusion | flops 1610678272 | bytes 9701380 | tf_op jit(solution)/shard_map/while/body/eval_jaxpr/dot_general | solution.py:50
  407.5 11.1 %fusion.37 = (f32[512]{0:T(512)S(1)}, f32[512,4096]{1,0:T(8,128)S(1)}) fusion(f32[64,4096]{1,0:T(8,128)S(1)} %get-tuple-element.271, f32[1,64,512]{2,0,1:T(1,128)S(1)} %constant_dynamic-slice_fusion.10, f32[4096]{0:T(1024)S(1)} %get-tuple-element.270, f32[512]{0:T(512)S(1)} %multiply_reduce_fusion.7, f32[4,512,4096]{2,1,0:T(8,128)} %get-tuple-element.269, ...), kind=kOutput, calls=%fused_computation.45.clone.1 | convolution fusion | flops 1623195136 | bytes 17977348 | tf_op jit(solution)/shard_map/while/body/eval_jaxpr/dot_general | solution.py:39
  418.7 8.2 %fusion.38 = f32[4,64,512]{2,1,0:T(8,128)S(1)} fusion(f32[4,64,512]{2,1,0:T(8,128)S(1)} %get-tuple-element.260, s32[]{:T(128)} %get-tuple-element.259, f32[512,4096]{1,0:T(8,128)S(1)} %get-tuple-element.240, f32[64,4096]{1,0:T(8,128)S(1)} %get-tuple-element.271, f32[1,64,512]{2,0,1:T(1,128)S(1)} %constant_dynamic-slice_fusion.10, ...), kind=kOutput, calls=%fused_computation.4.clone.1 | convolution fusion | flops 1610678272 | bytes 9701380 | tf_op jit(solution)/shard_map/while/body/eval_jaxpr/dot_general | solution.py:50
  426.9 0.1 constant_dynamic-slice_fusion.10
  427.1 11.1 %fusion.37 = (f32[512]{0:T(512)S(1)}, f32[512,4096]{1,0:T(8,128)S(1)}) fusion(f32[64,4096]{1,0:T(8,128)S(1)} %get-tuple-element.271, f32[1,64,512]{2,0,1:T(1,128)S(1)} %constant_dynamic-slice_fusion.10, f32[4096]{0:T(1024)S(1)} %get-tuple-element.270, f32[512]{0:T(512)S(1)} %multiply_reduce_fusion.7, f32[4,512,4096]{2,1,0:T(8,128)} %get-tuple-element.269, ...), kind=kOutput, calls=%fused_computation.45.clone.1 | convolution fusion | flops 1623195136 | bytes 17977348 | tf_op jit(solution)/shard_map/while/body/eval_jaxpr/dot_general | solution.py:39
  438.3 8.2 %fusion.38 = f32[4,64,512]{2,1,0:T(8,128)S(1)} fusion(f32[4,64,512]{2,1,0:T(8,128)S(1)} %get-tuple-element.260, s32[]{:T(128)} %get-tuple-element.259, f32[512,4096]{1,0:T(8,128)S(1)} %get-tuple-element.240, f32[64,4096]{1,0:T(8,128)S(1)} %get-tuple-element.271, f32[1,64,512]{2,0,1:T(1,128)S(1)} %constant_dynamic-slice_fusion.10, ...), kind=kOutput, calls=%fused_computation.4.clone.1 | convolution fusion | flops 1610678272 | bytes 9701380 | tf_op jit(solution)/shard_map/while/body/eval_jaxpr/dot_general | solution.py:50
  446.5 0.8 copy.36
  447.4 21.9 %reduce-scatter.3.cloned.1.call-done = f32[64,512]{1,0:T(8,128)} async-done(((f32[64,2048]{1,0:T(8,128)}), f32[64,512]{1,0:T(8,128)}) %reduce-scatter.3.cloned.1.call-update) | async-done | bytes 131088 | tf_op jit(solution)/shard_map/reduce_scatter | solution.py:92
  469.3 1.6 broadcast_multiply_fusion.1
  471.0 62.4 %all-gather.8.cloned.1.call-done = f32[64,16384]{1,0:T(8,128)} async-done(((f32[64,512]{1,0:T(8,128)}), f32[64,16384]{1,0:T(8,128)}) %all-gather.8.cloned.1.call-update) | async-done | bytes 4194320 | tf_op jit(solution)/shard_map/all_gather | solution.py:85
  533.4 1.1 constant_dynamic-slice_fusion.3
  534.5 0.4 reshape.37
  534.8 1.4 multiply_reduce_fusion.3
  536.3 98.9 %while.23 = (s32[]{:T(128)}, f32[4,64,512]{2,1,0:T(8,128)S(1)}, f32[4,512]{1,0:T(4,128)S(1)}, f32[4,64,512]{2,0,1:T(4,128)S(1)}, f32[4,512,4096]{2,1,0:T(8,128)}...) while((s32[]{:T(128)}, f32[4,64,512]{2,1,0:T(8,128)S(1)}, ...), condition=%wide.region_13.14_spmd, body=%wide.region_9.13_spmd.sunk | while | flops 3242326528 | bytes 36469864 | solution.py:61
  536.7 13.9 %fusion.41 = (f32[512]{0:T(512)S(1)}, f32[512]{0:T(512)S(1)}, f32[512,4096]{1,0:T(8,128)S(1)}) fusion(f32[4,512,4096]{2,1,0:T(8,128)} %get-tuple-element.295, s32[]{:T(128)} %get-tuple-element.282, f32[64,4096]{1,0:T(8,128)S(1)} %get-tuple-element.297, f32[1,64,512]{2,0,1:T(1,128)S(1)} %constant_dynamic-slice_fusion.11, ...), kind=kOutput, calls=%fused_computation.11.clone.1 | convolution fusion | flops 1629486080 | bytes 17979396 | tf_op jit(solution)/shard_map/while/body/eval_jaxpr/dot_general | solution.py:39
  550.6 10.5 %fusion.42 = f32[4,64,512]{2,1,0:T(8,128)S(1)} fusion(f32[4,64,512]{2,1,0:T(8,128)S(1)} %get-tuple-element.283, s32[]{:T(128)} %get-tuple-element.282, f32[64,4096]{1,0:T(8,128)S(1)} %get-tuple-element.297, f32[1,64,512]{2,0,1:T(1,128)S(1)} %constant_dynamic-slice_fusion.11, f32[512]{0:T(512)S(1)} %get-tuple-element.249, ...), kind=kOutput, calls=%fused_computation.16.clone.1 | convolution fusion | flops 1612775424 | bytes 18091008 | tf_op jit(solution)/shard_map/while/body/eval_jaxpr/dot_general | solution.py:50
  561.4 13.9 %fusion.41 = (f32[512]{0:T(512)S(1)}, f32[512]{0:T(512)S(1)}, f32[512,4096]{1,0:T(8,128)S(1)}) fusion(f32[4,512,4096]{2,1,0:T(8,128)} %get-tuple-element.295, s32[]{:T(128)} %get-tuple-element.282, f32[64,4096]{1,0:T(8,128)S(1)} %get-tuple-element.297, f32[1,64,512]{2,0,1:T(1,128)S(1)} %constant_dynamic-slice_fusion.11, ...), kind=kOutput, calls=%fused_computation.11.clone.1 | convolution fusion | flops 1629486080 | bytes 17979396 | tf_op jit(solution)/shard_map/while/body/eval_jaxpr/dot_general | solution.py:39
  575.3 10.5 %fusion.42 = f32[4,64,512]{2,1,0:T(8,128)S(1)} fusion(f32[4,64,512]{2,1,0:T(8,128)S(1)} %get-tuple-element.283, s32[]{:T(128)} %get-tuple-element.282, f32[64,4096]{1,0:T(8,128)S(1)} %get-tuple-element.297, f32[1,64,512]{2,0,1:T(1,128)S(1)} %constant_dynamic-slice_fusion.11, f32[512]{0:T(512)S(1)} %get-tuple-element.249, ...), kind=kOutput, calls=%fused_computation.16.clone.1 | convolution fusion | flops 1612775424 | bytes 18091008 | tf_op jit(solution)/shard_map/while/body/eval_jaxpr/dot_general | solution.py:50
  586.0 13.9 %fusion.41 = (f32[512]{0:T(512)S(1)}, f32[512]{0:T(512)S(1)}, f32[512,4096]{1,0:T(8,128)S(1)}) fusion(f32[4,512,4096]{2,1,0:T(8,128)} %get-tuple-element.295, s32[]{:T(128)} %get-tuple-element.282, f32[64,4096]{1,0:T(8,128)S(1)} %get-tuple-element.297, f32[1,64,512]{2,0,1:T(1,128)S(1)} %constant_dynamic-slice_fusion.11, ...), kind=kOutput, calls=%fused_computation.11.clone.1 | convolution fusion | flops 1629486080 | bytes 17979396 | tf_op jit(solution)/shard_map/while/body/eval_jaxpr/dot_general | solution.py:39
  599.9 10.5 %fusion.42 = f32[4,64,512]{2,1,0:T(8,128)S(1)} fusion(f32[4,64,512]{2,1,0:T(8,128)S(1)} %get-tuple-element.283, s32[]{:T(128)} %get-tuple-element.282, f32[64,4096]{1,0:T(8,128)S(1)} %get-tuple-element.297, f32[1,64,512]{2,0,1:T(1,128)S(1)} %constant_dynamic-slice_fusion.11, f32[512]{0:T(512)S(1)} %get-tuple-element.249, ...), kind=kOutput, calls=%fused_computation.16.clone.1 | convolution fusion | flops 1612775424 | bytes 18091008 | tf_op jit(solution)/shard_map/while/body/eval_jaxpr/dot_general | solution.py:50
  610.7 13.9 %fusion.41 = (f32[512]{0:T(512)S(1)}, f32[512]{0:T(512)S(1)}, f32[512,4096]{1,0:T(8,128)S(1)}) fusion(f32[4,512,4096]{2,1,0:T(8,128)} %get-tuple-element.295, s32[]{:T(128)} %get-tuple-element.282, f32[64,4096]{1,0:T(8,128)S(1)} %get-tuple-element.297, f32[1,64,512]{2,0,1:T(1,128)S(1)} %constant_dynamic-slice_fusion.11, ...), kind=kOutput, calls=%fused_computation.11.clone.1 | convolution fusion | flops 1629486080 | bytes 17979396 | tf_op jit(solution)/shard_map/while/body/eval_jaxpr/dot_general | solution.py:39
  624.6 10.5 %fusion.42 = f32[4,64,512]{2,1,0:T(8,128)S(1)} fusion(f32[4,64,512]{2,1,0:T(8,128)S(1)} %get-tuple-element.283, s32[]{:T(128)} %get-tuple-element.282, f32[64,4096]{1,0:T(8,128)S(1)} %get-tuple-element.297, f32[1,64,512]{2,0,1:T(1,128)S(1)} %constant_dynamic-slice_fusion.11, f32[512]{0:T(512)S(1)} %get-tuple-element.249, ...), kind=kOutput, calls=%fused_computation.16.clone.1 | convolution fusion | flops 1612775424 | bytes 18091008 | tf_op jit(solution)/shard_map/while/body/eval_jaxpr/dot_general | solution.py:50
  635.2 0.8 copy.37
  636.0 0.6 dynamic-slice
  637.3 10.5 %all-reduce = f32[2048]{0:T(1024)S(1)} all-reduce(f32[2048]{0:T(1024)S(1)} %bitcast.124), channel_id=4, replica_groups=mesh['row'=8,'col'=4] {'col'}, use_global_device_ids=true, to_apply=%region_15.16.clone | all-reduce | flops 2048 | bytes 16384
  647.8 1.3 fusion.14
  649.1 38.3 %all-reduce.1 = (f32[]{:T(128)}, f32[]{:T(128)}) all-reduce(f32[]{:T(128)} %get-tuple-element.147, f32[]{:T(128)} %get-tuple-element.156), channel_id=1, replica_groups=mesh['row'=8,'col'=4] {'row','col'}, use_global_device_ids=true, to_apply=%region_17.18 | all-reduce | flops 2 | bytes 16 | tf_op jit(solution)/shard_map/psum | solution.py:98
  688.7 1.6 broadcast_multiply_fusion
  (37 shorter events, 1.6 us)
Async XLA Ops:
  7.2 85.9 %all-gather.6.cloned.1.call-start = ((), (), s32[]{:S(2)}) async-start(), calls=%async_computation.3 | async-start | bytes 5242880 | tf_op jit(solution)/shard_map/all_gather | solution.py:74
  7.9 148.6 %all-gather.4.cloned.1.call-start = ((), (), s32[]{:S(2)}) async-start(), calls=%async_computation.2 | async-start | bytes 4325376 | tf_op jit(solution)/shard_map/all_gather | solution.py:85
  8.6 276.9 %all-reduce.5.cloned.1.call-start = ((), (), s32[]{:S(2)}) async-start(), calls=%async_computation.7 | async-start | bytes 16777216 | tf_op jit(solution)/shard_map/psum | solution.py:13
  99.0 370.3 %reduce-scatter.3.cloned.1.call-start = ((), (), s32[]{:S(2)}) async-start(), calls=%async_computation.4 | async-start | bytes 655360 | tf_op jit(solution)/shard_map/reduce_scatter | solution.py:92
  285.5 5.3 copy-start
  447.4 86.0 %all-gather.8.cloned.1.call-start = ((), (), s32[]{:S(2)}) async-start(), calls=%async_computation.5 | async-start | bytes 4325376 | tf_op jit(solution)/shard_map/all_gather | solution.py:85
  470.9 217.8 %reduce-scatter.5.cloned.1.call-start = ((), (), s32[]{:S(2)}) async-start(), calls=%async_computation.6 | async-start | bytes 655360 | tf_op jit(solution)/shard_map/reduce_scatter | solution.py:92
  536.3 99.8 %copy-start.1 = (u32[32]{0:T(128)S(1)}, u32[32]{0:T(128)}, u32[]{:S(2)}) copy-start(u32[32]{0:T(128)} %constant.75) | copy-start | bytes 388
Sparse Core Ops, SparseCore 0:
  9.6 83.4 all-gather.5
  96.1 60.2 all-gather.3
  160.2 125.3 all-reduce.4
  447.5 21.7 reduce-scatter.2
  473.3 60.0 all-gather.7
  636.2 19.9 reduce-scatter.4
where the time goes:
time: 699 us; the launch traced here: 698 us
  waiting for transfers between devices  351 us (50%)
  matrix products  201 us (29%)
  blocking collectives  48.8 us (7%)
  other arithmetic  41.9 us (6%)
  local copies, waits for them, and re-layouts  37.5 us (5%)
  between operations  17.4 us (2%)
    psum x1, waiting for transfers between devices, from_root(): return lax.psum(block, axis)  126 us
    all_gather x2, waiting for transfers between devices, on_device(): everything = lax.all_gather(current, ('row', 'col'), axis=1, tiled=True)  117 us
    dot_general x8, matrix products, one_block(): lax.dot_general(x_blk, x_cols, (((0,), (0,)), ((), ())), precision=EXACT,...  100 us
    all_gather x1, waiting for transfers between devices, on_device(): feature_rows = lax.all_gather(features, 'col', axis=0, tiled=True)  84.4 us
    dot_general x8, matrix products, one_block(): lax.dot_general(x_cols, ratios, (((1,), (1,)), ((), ())), precision=EXACT...  74.9 us
    psum x1, blocking collectives, on_device(): lax.psum((local_stress, dissim_sq), ('row', 'col'))  38.3 us
    while x1, local copies, waits for them, and re-layouts, guttman_terms(): pull_terms, stress = lax.map(one_block, (dis_blocks, x_blocks))  31.1 us
    dot_general x2, matrix products, tanimoto(): lax.dot_general(left_rows, right_rows, (((1,), (1,)), ((), ())), preferre...  25.8 us
  transfers between devices with their start and end apart: 6, of which 5 were waited for; matrix products, arithmetic and copies ran while one was open for 2% of the time, Pallas kernels for 0%

commit v1 on v0

--- a/solution.py
+++ b/solution.py
@@ -6,6 +6,19 @@
 ITERS = 2
 FLOOR = 0.25
 EXACT = lax.Precision.HIGHEST
+
+
+def ring_gather(x, axis, dim):
+    ways = lax.axis_size(axis)
+    up = [(d, (d + 1) % ways) for d in range(ways)]
+    down = [(d, (d - 1) % ways) for d in range(ways)]
+    earlier, later = ([x], [x])
+    for _ in range(ways // 2):
+        earlier.append(lax.ppermute(earlier[-1], axis, up))
+    for _ in range((ways - 1) // 2):
+        later.append(lax.ppermute(later[-1], axis, down))
+    line = jnp.concatenate([*earlier[::-1], *later[1:]], axis=dim)
+    return jnp.roll(line, (lax.axis_index(axis) - ways // 2) * x.shape[dim], axis=dim)
 
 
 def from_root(block, axis, owner):
@@ -71,7 +84,7 @@
     share_len = coords.shape[1]
     row_len = share_len * cols_n
     molecules = row_len * rows_n
-    feature_rows = lax.all_gather(features, "col", axis=0, tiled=True)
+    feature_rows = ring_gather(features, "col", 0)
     rows_sq = squares_of(feature_rows)
     pieces = []
     for offset in range(ratio_k):

time: 699 us -> 647 us (0.926)
  waiting for transfers between devices: 351 us -> 276 us
  local copies, waits for them, and re-layouts: 37.5 us -> 44.9 us
    all_gather x1 -> x0, waiting for transfers between devices: 84.4 us -> none  [on_device(): feature_rows = lax.all_gather(features, 'col', axis=0, tiled=True)]
    ppermute x0 -> x3, waiting for transfers between devices: none -> 65.9 us  [the longest x2 49.6 us: ring_gather(): earlier.append(lax.ppermute(earlier[-1], axis, up))]
    all_gather x2, waiting for transfers between devices: 117 us -> 60.2 us  [on_device(): everything = lax.all_gather(current, ('row', 'col'), axis=1, tiled=True)]
    unnamed x6 -> x19, local copies, waits for them, and re-layouts: 0.6 us -> 7.99 us
  transfers between devices with their start and end apart: 6 -> 8, of which waited for: 5 -> 6; matrix products, arithmetic and copies ran while one was open for 2% -> 14% of each run, Pallas kernels for 0% -> 0%
where the time goes in v1:
time: 647 us; the launch traced here: 641 us
  waiting for transfers between devices  276 us (43%)
  matrix products  204 us (32%)
  blocking collectives  48.9 us (8%)
  local copies, waits for them, and re-layouts  44.9 us (7%)
  other arithmetic  41.1 us (6%)
  between operations  18.8 us (3%)
  starting transfers between devices  7.11 us (1%)
    psum x1, waiting for transfers between devices, from_root(): return lax.psum(block, axis)  128 us
    dot_general x8, matrix products, one_block(): lax.dot_general(x_blk, x_cols, (((0,), (0,)), ((), ())), precision=EXACT,...  100 us
    dot_general x8, matrix products, one_block(): lax.dot_general(x_cols, ratios, (((1,), (1,)), ((), ())), precision=EXACT...  74.9 us
    all_gather x2, waiting for transfers between devices, on_device(): everything = lax.all_gather(current, ('row', 'col'), axis=1, tiled=True)  60.2 us
    ppermute x2, waiting for transfers between devices, ring_gather(): earlier.append(lax.ppermute(earlier[-1], axis, up))  49.6 us
    psum x1, blocking collectives, on_device(): lax.psum((local_stress, dissim_sq), ('row', 'col'))  38.2 us
    while x1, local copies, waits for them, and re-layouts, guttman_terms(): pull_terms, stress = lax.map(one_block, (dis_blocks, x_blocks))  31.1 us
    dot_general x2, matrix products, tanimoto(): lax.dot_general(left_rows, right_rows, (((1,), (1,)), ((), ())), preferre...  28.3 us
  transfers between devices with their start and end apart: 8, of which 6 were waited for; matrix products, arithmetic and copies ran while one was open for 14% of the time, Pallas kernels for 0%

profile of v1, /device:TPU:0, one launch (start us, length us, event | category | flops | bytes accessed | tf_op | source)
XLA Modules:
  0.0 641.2 jit_solution(17934331471184371748)
XLA Ops:
  8.1 3.1 collective-permute-start
  11.1 25.4 %collective-permute-done = bf16[512,1024]{1,0:T(8,128)(2,1)S(1)} collective-permute-done((bf16[512,1024]{1,0:T(8,128)(2,1)}, bf16[512,1024]{1,0:T(8,128)(2,1)S(1)}, u32[]{:S(2)}, u32[]{:S(2)}) %collective-permute-start) | collective-permute-done | bytes 1048608 | tf_op jit(solution)/shard_map/ppermute | solution.py:17
  36.5 3.8 collective-permute-start.2
  40.4 24.2 %collective-permute-done.1 = bf16[512,1024]{1,0:T(8,128)(2,1)} collective-permute-done((bf16[512,1024]{1,0:T(8,128)(2,1)S(1)}, bf16[512,1024]{1,0:T(8,128)(2,1)}, u32[]{:S(2)}, u32[]{:S(2)}) %collective-permute-start.1) | collective-permute-done | bytes 1048608 | tf_op jit(solution)/shard_map/ppermute | solution.py:17
  64.5 1.3 constant_dynamic-update-slice_fusion.7
  65.9 1.3 constant_dynamic-update-slice_fusion.5
  67.2 16.4 %collective-permute-done.2 = bf16[512,1024]{1,0:T(8,128)(2,1)S(1)} collective-permute-done((bf16[512,1024]{1,0:T(8,128)(2,1)}, bf16[512,1024]{1,0:T(8,128)(2,1)S(1)}, u32[]{:S(2)}, u32[]{:S(2)}) %collective-permute-start.2) | collective-permute-done | bytes 1048608 | tf_op jit(solution)/shard_map/ppermute | solution.py:19
  83.6 1.3 constant_dynamic-update-slice_fusion.3
  85.2 3.2 copy-done
  88.4 5.0 broadcast_select_fusion.1
  94.1 3.1 fusion.13
  97.2 127.6 %all-reduce.5.cloned.1.call-done = (bf16[2048,1024]{1,0:T(8,128)(2,1)}, bf16[2048,1024]{1,0:T(8,128)(2,1)}) async-done(((bf16[2048,1024]{1,0:T(8,128)(2,1)}, bf16[2048,1024]{1,0:T(8,128)(2,1)}), (bf16[2048,1024]{1,0:T(8,128)(2,1)}, bf16[2048,1024]{1,0:T(8,128)(2,1)})) %all-reduce.5.cloned.1.call-update) | async-done | bytes 8388624 | tf_op jit(solution)/shard_map/psum | solution.py:26
  224.8 5.3 fusion.11
  230.1 13.9 %fusion.9 = f32[2048,2048]{0,1:T(8,128)S(1)} fusion(f32[2048]{0:T(1024)S(1)} %get-tuple-element.161, f32[2048]{0:T(1024)S(1)} %fusion.13, bf16[2048,1024]{1,0:T(8,128)(2,1)} %get-tuple-element.146, bf16[4096,1024]{1,0:T(8,128)(2,1)} %copy-done, s32[]{:T(128)S(6)} %select_n.37), kind=kOutput, calls=%fused_computation.25 | convolution fusion | flops 8606711808 | bytes 25182212 | tf_op jit(solution)/shard_map/dot_general | solution.py:35
  244.1 14.4 %fusion.10 = f32[2048,2048]{0,1:T(8,128)} fusion(f32[2048]{0:T(1024)S(1)} %get-tuple-element.160, f32[2048]{0:T(1024)S(1)} %fusion.13, bf16[2048,1024]{1,0:T(8,128)(2,1)} %get-tuple-element.145, bf16[4096,1024]{1,0:T(8,128)(2,1)S(1)} %bitcast.112, s32[]{:T(128)S(6)} %select_n.37), kind=kOutput, calls=%fused_computation.26 | convolution fusion | flops 8606711808 | bytes 25182212 | tf_op jit(solution)/shard_map/dot_general | solution.py:35
  258.5 20.3 %multiply_reduce_fusion.2 = (f32[]{:T(128)}, f32[2048,4096]{0,1:T(8,128)}) fusion(f32[2048,2048]{0,1:T(8,128)} %fusion.10, f32[2048,2048]{0,1:T(8,128)S(1)} %fusion.9), kind=kLoop, calls=%fused_computation.22 | loop fusion | flops 25165824 | bytes 67108864 | tf_op jit(solution)/shard_map/reduce_sum | solution.py:94
  278.8 31.1 %copy.33 = f32[2048,4096]{1,0:T(8,128)} copy(f32[2048,4096]{0,1:T(8,128)} %get-tuple-element.157) | data formatting | bytes 67108864 | tf_op jit(solution)/shard_map/while | solution.py:74
  309.9 1.1 constant_dynamic-slice_fusion.5
  311.3 1.4 multiply_reduce_fusion.4
  312.7 78.4 %while.22 = (s32[]{:T(128)}, f32[4,64,512]{2,1,0:T(8,128)S(1)}, f32[4,64,512]{2,0,1:T(4,128)S(1)}, f32[4,512,4096]{2,1,0:T(8,128)}, f32[4096]{0:T(1024)S(1)}, /*index=5*/f32[64,4096]{1,0:T(8,128)S(1)}, s32[]{:T(128)}) while((s32[]{:T(128)}, f32[4,64,512]{2,1,0:T(8,128)S(1)}, f32[4,64,512]{2,0,1:T(4,128)S(1)}, f32[4,512,4096]{2,1,0:T(8,128)}, ...), condition=%wide.region_6.7_spmd, body=%wide.region_3.6_spmd.sunk | while | flops 3233938432 | bytes 28074072 | solution.py:74
  313.1 11.2 %fusion.39 = (f32[512]{0:T(512)S(1)}, f32[512,4096]{1,0:T(8,128)S(1)}) fusion(f32[64,4096]{1,0:T(8,128)S(1)} %get-tuple-element.271, f32[1,64,512]{2,0,1:T(1,128)S(1)} %constant_dynamic-slice_fusion.10, f32[4096]{0:T(1024)S(1)} %get-tuple-element.270, f32[512]{0:T(512)S(1)} %multiply_reduce_fusion.7, f32[4,512,4096]{2,1,0:T(8,128)} %get-tuple-element.269, ...), kind=kOutput, calls=%fused_computation.57.clone.1 | convolution fusion | flops 1623195136 | bytes 17977348 | tf_op jit(solution)/shard_map/while/body/eval_jaxpr/dot_general | solution.py:52
  324.2 8.2 %fusion.40 = f32[4,64,512]{2,1,0:T(8,128)S(1)} fusion(f32[4,64,512]{2,1,0:T(8,128)S(1)} %get-tuple-element.260, s32[]{:T(128)} %get-tuple-element.259, f32[512,4096]{1,0:T(8,128)S(1)} %get-tuple-element.240, f32[64,4096]{1,0:T(8,128)S(1)} %get-tuple-element.271, f32[1,64,512]{2,0,1:T(1,128)S(1)} %constant_dynamic-slice_fusion.10, ...), kind=kOutput, calls=%fused_computation.4.clone.1 | convolution fusion | flops 1610678272 | bytes 9701380 | tf_op jit(solution)/shard_map/while/body/eval_jaxpr/dot_general | solution.py:63
  332.6 11.1 %fusion.39 = (f32[512]{0:T(512)S(1)}, f32[512,4096]{1,0:T(8,128)S(1)}) fusion(f32[64,4096]{1,0:T(8,128)S(1)} %get-tuple-element.271, f32[1,64,512]{2,0,1:T(1,128)S(1)} %constant_dynamic-slice_fusion.10, f32[4096]{0:T(1024)S(1)} %get-tuple-element.270, f32[512]{0:T(512)S(1)} %multiply_reduce_fusion.7, f32[4,512,4096]{2,1,0:T(8,128)} %get-tuple-element.269, ...), kind=kOutput, calls=%fused_computation.57.clone.1 | convolution fusion | flops 1623195136 | bytes 17977348 | tf_op jit(solution)/shard_map/while/body/eval_jaxpr/dot_general | solution.py:52
  343.8 8.2 %fusion.40 = f32[4,64,512]{2,1,0:T(8,128)S(1)} fusion(f32[4,64,512]{2,1,0:T(8,128)S(1)} %get-tuple-element.260, s32[]{:T(128)} %get-tuple-element.259, f32[512,4096]{1,0:T(8,128)S(1)} %get-tuple-element.240, f32[64,4096]{1,0:T(8,128)S(1)} %get-tuple-element.271, f32[1,64,512]{2,0,1:T(1,128)S(1)} %constant_dynamic-slice_fusion.10, ...), kind=kOutput, calls=%fused_computation.4.clone.1 | convolution fusion | flops 1610678272 | bytes 9701380 | tf_op jit(solution)/shard_map/while/body/eval_jaxpr/dot_general | solution.py:63
  352.2 11.1 %fusion.39 = (f32[512]{0:T(512)S(1)}, f32[512,4096]{1,0:T(8,128)S(1)}) fusion(f32[64,4096]{1,0:T(8,128)S(1)} %get-tuple-element.271, f32[1,64,512]{2,0,1:T(1,128)S(1)} %constant_dynamic-slice_fusion.10, f32[4096]{0:T(1024)S(1)} %get-tuple-element.270, f32[512]{0:T(512)S(1)} %multiply_reduce_fusion.7, f32[4,512,4096]{2,1,0:T(8,128)} %get-tuple-element.269, ...), kind=kOutput, calls=%fused_computation.57.clone.1 | convolution fusion | flops 1623195136 | bytes 17977348 | tf_op jit(solution)/shard_map/while/body/eval_jaxpr/dot_general | solution.py:52
  363.3 8.2 %fusion.40 = f32[4,64,512]{2,1,0:T(8,128)S(1)} fusion(f32[4,64,512]{2,1,0:T(8,128)S(1)} %get-tuple-element.260, s32[]{:T(128)} %get-tuple-element.259, f32[512,4096]{1,0:T(8,128)S(1)} %get-tuple-element.240, f32[64,4096]{1,0:T(8,128)S(1)} %get-tuple-element.271, f32[1,64,512]{2,0,1:T(1,128)S(1)} %constant_dynamic-slice_fusion.10, ...), kind=kOutput, calls=%fused_computation.4.clone.1 | convolution fusion | flops 1610678272 | bytes 9701380 | tf_op jit(solution)/shard_map/while/body/eval_jaxpr/dot_general | solution.py:63
  371.8 11.1 %fusion.39 = (f32[512]{0:T(512)S(1)}, f32[512,4096]{1,0:T(8,128)S(1)}) fusion(f32[64,4096]{1,0:T(8,128)S(1)} %get-tuple-element.271, f32[1,64,512]{2,0,1:T(1,128)S(1)} %constant_dynamic-slice_fusion.10, f32[4096]{0:T(1024)S(1)} %get-tuple-element.270, f32[512]{0:T(512)S(1)} %multiply_reduce_fusion.7, f32[4,512,4096]{2,1,0:T(8,128)} %get-tuple-element.269, ...), kind=kOutput, calls=%fused_computation.57.clone.1 | convolution fusion | flops 1623195136 | bytes 17977348 | tf_op jit(solution)/shard_map/while/body/eval_jaxpr/dot_general | solution.py:52
  382.9 8.2 %fusion.40 = f32[4,64,512]{2,1,0:T(8,128)S(1)} fusion(f32[4,64,512]{2,1,0:T(8,128)S(1)} %get-tuple-element.260, s32[]{:T(128)} %get-tuple-element.259, f32[512,4096]{1,0:T(8,128)S(1)} %get-tuple-element.240, f32[64,4096]{1,0:T(8,128)S(1)} %get-tuple-element.271, f32[1,64,512]{2,0,1:T(1,128)S(1)} %constant_dynamic-slice_fusion.10, ...), kind=kOutput, calls=%fused_computation.4.clone.1 | convolution fusion | flops 1610678272 | bytes 9701380 | tf_op jit(solution)/shard_map/while/body/eval_jaxpr/dot_general | solution.py:63
  391.2 0.8 copy.36
  392.1 21.9 %reduce-scatter.3.cloned.1.call-done = f32[64,512]{1,0:T(8,128)} async-done(((f32[64,2048]{1,0:T(8,128)}), f32[64,512]{1,0:T(8,128)}) %reduce-scatter.3.cloned.1.call-update) | async-done | bytes 131088 | tf_op jit(solution)/shard_map/reduce_scatter | solution.py:105
  414.0 1.6 broadcast_multiply_fusion.1
  415.7 60.2 %all-gather.5.cloned.1.call-done = f32[64,16384]{1,0:T(8,128)} async-done(((f32[64,512]{1,0:T(8,128)}), f32[64,16384]{1,0:T(8,128)}) %all-gather.5.cloned.1.call-update) | async-done | bytes 4194320 | tf_op jit(solution)/shard_map/all_gather | solution.py:98
  475.8 1.1 constant_dynamic-slice_fusion.3
  477.3 1.4 multiply_reduce_fusion.3
  478.7 98.8 %while.23 = (s32[]{:T(128)}, f32[4,64,512]{2,1,0:T(8,128)S(1)}, f32[4,512]{1,0:T(4,128)S(1)}, f32[4,64,512]{2,0,1:T(4,128)S(1)}, f32[4,512,4096]{2,1,0:T(8,128)}...) while((s32[]{:T(128)}, f32[4,64,512]{2,1,0:T(8,128)S(1)}, ...), condition=%wide.region_13.14_spmd, body=%wide.region_9.13_spmd.sunk | while | flops 3242326528 | bytes 36469864 | solution.py:74
  479.1 13.9 %fusion.43 = (f32[512]{0:T(512)S(1)}, f32[512]{0:T(512)S(1)}, f32[512,4096]{1,0:T(8,128)S(1)}) fusion(f32[4,512,4096]{2,1,0:T(8,128)} %get-tuple-element.295, s32[]{:T(128)} %get-tuple-element.282, f32[64,4096]{1,0:T(8,128)S(1)} %get-tuple-element.297, f32[1,64,512]{2,0,1:T(1,128)S(1)} %constant_dynamic-slice_fusion.11, ...), kind=kOutput, calls=%fused_computation.11.clone.1 | convolution fusion | flops 1629486080 | bytes 17979396 | tf_op jit(solution)/shard_map/while/body/eval_jaxpr/dot_general | solution.py:52
  493.0 10.5 %fusion.44 = f32[4,64,512]{2,1,0:T(8,128)S(1)} fusion(f32[4,64,512]{2,1,0:T(8,128)S(1)} %get-tuple-element.283, s32[]{:T(128)} %get-tuple-element.282, f32[64,4096]{1,0:T(8,128)S(1)} %get-tuple-element.297, f32[1,64,512]{2,0,1:T(1,128)S(1)} %constant_dynamic-slice_fusion.11, f32[512]{0:T(512)S(1)} %get-tuple-element.249, ...), kind=kOutput, calls=%fused_computation.16.clone.1 | convolution fusion | flops 1612775424 | bytes 18091008 | tf_op jit(solution)/shard_map/while/body/eval_jaxpr/dot_general | solution.py:63
  503.8 13.9 %fusion.43 = (f32[512]{0:T(512)S(1)}, f32[512]{0:T(512)S(1)}, f32[512,4096]{1,0:T(8,128)S(1)}) fusion(f32[4,512,4096]{2,1,0:T(8,128)} %get-tuple-element.295, s32[]{:T(128)} %get-tuple-element.282, f32[64,4096]{1,0:T(8,128)S(1)} %get-tuple-element.297, f32[1,64,512]{2,0,1:T(1,128)S(1)} %constant_dynamic-slice_fusion.11, ...), kind=kOutput, calls=%fused_computation.11.clone.1 | convolution fusion | flops 1629486080 | bytes 17979396 | tf_op jit(solution)/shard_map/while/body/eval_jaxpr/dot_general | solution.py:52
  517.7 10.5 %fusion.44 = f32[4,64,512]{2,1,0:T(8,128)S(1)} fusion(f32[4,64,512]{2,1,0:T(8,128)S(1)} %get-tuple-element.283, s32[]{:T(128)} %get-tuple-element.282, f32[64,4096]{1,0:T(8,128)S(1)} %get-tuple-element.297, f32[1,64,512]{2,0,1:T(1,128)S(1)} %constant_dynamic-slice_fusion.11, f32[512]{0:T(512)S(1)} %get-tuple-element.249, ...), kind=kOutput, calls=%fused_computation.16.clone.1 | convolution fusion | flops 1612775424 | bytes 18091008 | tf_op jit(solution)/shard_map/while/body/eval_jaxpr/dot_general | solution.py:63
  528.4 13.9 %fusion.43 = (f32[512]{0:T(512)S(1)}, f32[512]{0:T(512)S(1)}, f32[512,4096]{1,0:T(8,128)S(1)}) fusion(f32[4,512,4096]{2,1,0:T(8,128)} %get-tuple-element.295, s32[]{:T(128)} %get-tuple-element.282, f32[64,4096]{1,0:T(8,128)S(1)} %get-tuple-element.297, f32[1,64,512]{2,0,1:T(1,128)S(1)} %constant_dynamic-slice_fusion.11, ...), kind=kOutput, calls=%fused_computation.11.clone.1 | convolution fusion | flops 1629486080 | bytes 17979396 | tf_op jit(solution)/shard_map/while/body/eval_jaxpr/dot_general | solution.py:52
  542.3 10.5 %fusion.44 = f32[4,64,512]{2,1,0:T(8,128)S(1)} fusion(f32[4,64,512]{2,1,0:T(8,128)S(1)} %get-tuple-element.283, s32[]{:T(128)} %get-tuple-element.282, f32[64,4096]{1,0:T(8,128)S(1)} %get-tuple-element.297, f32[1,64,512]{2,0,1:T(1,128)S(1)} %constant_dynamic-slice_fusion.11, f32[512]{0:T(512)S(1)} %get-tuple-element.249, ...), kind=kOutput, calls=%fused_computation.16.clone.1 | convolution fusion | flops 1612775424 | bytes 18091008 | tf_op jit(solution)/shard_map/while/body/eval_jaxpr/dot_general | solution.py:63
  553.1 13.9 %fusion.43 = (f32[512]{0:T(512)S(1)}, f32[512]{0:T(512)S(1)}, f32[512,4096]{1,0:T(8,128)S(1)}) fusion(f32[4,512,4096]{2,1,0:T(8,128)} %get-tuple-element.295, s32[]{:T(128)} %get-tuple-element.282, f32[64,4096]{1,0:T(8,128)S(1)} %get-tuple-element.297, f32[1,64,512]{2,0,1:T(1,128)S(1)} %constant_dynamic-slice_fusion.11, ...), kind=kOutput, calls=%fused_computation.11.clone.1 | convolution fusion | flops 1629486080 | bytes 17979396 | tf_op jit(solution)/shard_map/while/body/eval_jaxpr/dot_general | solution.py:52
  567.0 10.5 %fusion.44 = f32[4,64,512]{2,1,0:T(8,128)S(1)} fusion(f32[4,64,512]{2,1,0:T(8,128)S(1)} %get-tuple-element.283, s32[]{:T(128)} %get-tuple-element.282, f32[64,4096]{1,0:T(8,128)S(1)} %get-tuple-element.297, f32[1,64,512]{2,0,1:T(1,128)S(1)} %constant_dynamic-slice_fusion.11, f32[512]{0:T(512)S(1)} %get-tuple-element.249, ...), kind=kOutput, calls=%fused_computation.16.clone.1 | convolution fusion | flops 1612775424 | bytes 18091008 | tf_op jit(solution)/shard_map/while/body/eval_jaxpr/dot_general | solution.py:63
  577.6 0.8 copy.37
  579.7 10.7 %all-reduce = f32[2048]{0:T(1024)S(1)} all-reduce(f32[2048]{0:T(1024)S(1)} %bitcast.120), channel_id=4, replica_groups=mesh['row'=8,'col'=4] {'col'}, use_global_device_ids=true, to_apply=%region_15.16.clone | all-reduce | flops 2048 | bytes 16384
  590.3 1.3 fusion.18
  591.6 38.2 %all-reduce.1 = (f32[]{:T(128)}, f32[]{:T(128)}) all-reduce(f32[]{:T(128)} %get-tuple-element.147, f32[]{:T(128)} %get-tuple-element.156), channel_id=1, replica_groups=mesh['row'=8,'col'=4] {'row','col'}, use_global_device_ids=true, to_apply=%region_17.18 | all-reduce | flops 2 | bytes 16 | tf_op jit(solution)/shard_map/psum | solution.py:111
  631.2 1.6 broadcast_multiply_fusion
  (55 shorter events, 3.9 us)
Async XLA Ops:
  8.0 77.0 %copy-start.1 = (bf16[512,1024]{1,0:T(8,128)(2,1)S(1)}, bf16[512,1024]{1,0:T(8,128)(2,1)}, u32[]{:S(2)}) copy-start(bf16[512,1024]{1,0:T(8,128)(2,1)} %param.6) | copy-start | bytes 3145732
  8.0 216.8 %all-reduce.5.cloned.1.call-start = ((), (), s32[]{:S(2)}) async-start(), calls=%async_computation.6 | async-start | bytes 16777216 | tf_op jit(solution)/shard_map/psum | solution.py:26
  8.1 28.5 %collective-permute-start = (bf16[512,1024]{1,0:T(8,128)(2,1)}, bf16[512,1024]{1,0:T(8,128)(2,1)S(1)}, u32[]{:S(2)}, u32[]{:S(2)}) collective-permute-start(bf16[512,1024]{1,0:T(8,128)(2,1)} %param.6), channel_id=1, source_target_pairs={{0,1},{1,2},{2,3},{3,0},{4,5},{5,6},{6,7},{7,4},{8,9},{9,10},{10,1... | collective-permute-start | bytes 3145736 | tf_op jit(solution)/shard_map/ppermute | solution.py:17
  36.5 28.0 %collective-permute-start.1 = (bf16[512,1024]{1,0:T(8,128)(2,1)S(1)}, bf16[512,1024]{1,0:T(8,128)(2,1)}, u32[]{:S(2)}, u32[]{:S(2)}) collective-permute-start(bf16[512,1024]{1,0:T(8,128)(2,1)S(1)} %collective-permute-done), channel_id=1, source_target_pairs={{0,1},{1,2},{2,3},{3,0},{4,5},{5,6},{6,7},{7,4},{8,9},{9,10},{10,1... | collective-permute-start | bytes 3145736 | tf_op jit(solution)/shard_map/ppermute | solution.py:17
  36.5 47.0 %collective-permute-start.2 = (bf16[512,1024]{1,0:T(8,128)(2,1)}, bf16[512,1024]{1,0:T(8,128)(2,1)S(1)}, u32[]{:S(2)}, u32[]{:S(2)}) collective-permute-start(bf16[512,1024]{1,0:T(8,128)(2,1)} %param.6), channel_id=1, source_target_pairs={{0,3},{1,0},{2,1},{3,2},{4,7},{5,4},{6,5},{7,6},{8,11},{9,8},{10,9... | collective-permute-start | bytes 3145736 | tf_op jit(solution)/shard_map/ppermute | solution.py:19
  85.2 3.2 copy-start
  93.5 216.4 %all-gather.3.cloned.1.call-start = ((), (), s32[]{:S(2)}) async-start(), calls=%async_computation.2 | async-start | bytes 4325376 | tf_op jit(solution)/shard_map/all_gather | solution.py:98
  94.0 320.0 %reduce-scatter.3.cloned.1.call-start = ((), (), s32[]{:S(2)}) async-start(), calls=%async_computation.3 | async-start | bytes 655360 | tf_op jit(solution)/shard_map/reduce_scatter | solution.py:105
  224.8 19.3 %slice-start = ((s8[8388608]{0:T(1024)(128)(4,1)}), s8[4194304]{0:T(1024)(128)(4,1)S(1)}, s32[]{:S(2)}) async-start(s8[8388608]{0:T(1024)(128)(4,1)} %bitcast.111), calls=%async_computation.7 | async-start | bytes 8388608
  230.1 14.0 %slice-start.1 = ((s8[8388608]{0:T(1024)(128)(4,1)}), s8[4194304]{0:T(1024)(128)(4,1)S(1)}, s32[]{:S(2)}) async-start(s8[8388608]{0:T(1024)(128)(4,1)} %bitcast.111), calls=%async_computation.8 | async-start | bytes 8388608
  392.0 83.8 %all-gather.5.cloned.1.call-start = ((), (), s32[]{:S(2)}) async-start(), calls=%async_computation.4 | async-start | bytes 4325376 | tf_op jit(solution)/shard_map/all_gather | solution.py:98
  415.6 215.6 %reduce-scatter.5.cloned.1.call-start = ((), (), s32[]{:S(2)}) async-start(), calls=%async_computation.5 | async-start | bytes 655360 | tf_op jit(solution)/shard_map/reduce_scatter | solution.py:105
  478.7 99.7 %copy-start.2 = (u32[32]{0:T(128)S(1)}, u32[32]{0:T(128)}, u32[]{:S(2)}) copy-start(u32[32]{0:T(128)} %constant.99) | copy-start | bytes 388
Sparse Core Ops, SparseCore 0:
  93.6 131.1 all-reduce.4
  392.1 21.8 reduce-scatter.2
  578.5 20.1 reduce-scatter.4
Sparse Core Ops, SparseCore 1:
  97.5 77.9 all-gather.2
  415.7 60.1 all-gather.4
